TPU v7x, 256 devices: a whole 4x4x8 slice. The times are simulated.
256 devices in a mesh: sub: 8 (over y, core), region: 32 (over z, x).
Axes of the slice: x: 4, y: 4, z: 8, core: 2. Of those that a mesh axis runs over, the one named last changes fastest.
Arguments:
- pieces: float32 [64, 32, 32, 512], P('sub', 'region'), may hold values from -6 to 6
- local_inverse: float32 [64, 32, 512, 512], P('sub', 'region'), may hold values from -0.25 to 0.25
- primal_basis: float32 [64, 32, 24, 512], P('sub', 'region'), may hold values from -0.25 to 0.25
- match_south: int32 [64, 32, 128], P('sub', 'region'), may hold values from 0 to 127, each once within a row
- match_east: int32 [64, 32, 128], P('sub', 'region'), may hold values from 0 to 127, each once within a row
- primal_index: int32 [64, 32, 24], P('sub', 'region'), may hold values from 0 to 383
- stiffness: int32 [64, 32], replicated, may hold values from 1 to 16
- level2_inverse: float32 [32, 384, 384], P('region', 'sub'), may hold values from -0.3125 to 0.3125
- level2_basis: float32 [32, 60, 384], P('region'), may hold values from -0.3125 to 0.3125
- top_inverse: float32 [1920, 1920], P(None, 'region'), as said below
Outputs:
- preconditioned: float32 [64, 32, 32, 512], P('sub', 'region')
Inputs may be any that keep to these rules, and one draw needn't show every extreme that they name: top_inverse is symmetric.
All inputs are finite; a program needn't handle non-finite values.
Results may differ from a plain program's by a relative error of at most 0.000053.
Values sent between devices are 32-bit elements; how exact they have to be, the bound alone decides.
A program may use at most 64 MiB of HBM per device.

v0:
```python
import jax
import jax.numpy as jnp
from jax import lax
from jax.sharding import PartitionSpec as P

B = 512
P2 = 60


HIGH = lax.Precision.HIGHEST


def padded_2(block, sides, width):
    for axis, dim in sides:
        count = lax.axis_size(axis)
        forward = [(i, i + 1) for i in range(count - 1)]
        backward = [(target, source) for source, target in forward]
        low = lax.ppermute(
            lax.slice_in_dim(block, block.shape[dim] - width, None, axis=dim), axis, forward
        )
        high = lax.ppermute(lax.slice_in_dim(block, 0, width, axis=dim), axis, backward)
        block = jnp.concatenate([low, block, high], axis=dim)
    return block


def permute_rows(values, table):
    return jnp.einsum("skx,sxj->skj", values, table, precision=HIGH)


def assemble(values, pick_south, pick_east, send_south, send_east):
    width = values.shape[-1] // 4
    north_face = values[..., :width]
    south_face = values[..., width : 2 * width]
    west_face = values[..., 2 * width : 3 * width]
    east_face = values[..., 3 * width :]
    sent_south = permute_rows(south_face, send_south)
    edges = jnp.stack([north_face[0], sent_south[-1]])
    extended = padded_2(edges, (("sub", 0),), 1)
    from_north = jnp.concatenate([extended[:1], sent_south[:-1]], axis=0)
    next_north = jnp.concatenate([north_face[1:], extended[3:]], axis=0)
    from_south = permute_rows(next_north, pick_south)
    sent_east = permute_rows(east_face, send_east)
    sides = jnp.stack([west_face, sent_east])
    widened = padded_2(sides, (("region", 0),), 1)
    from_west = widened[0]
    from_east = permute_rows(widened[3], pick_east)
    return values + jnp.concatenate([from_north, from_south, from_west, from_east], axis=-1)


def on_device(
    pieces,
    local_inverse,
    primal_basis,
    match_south,
    match_east,
    primal_index,
    stiffness,
    level2_inverse,
    level2_basis,
    top_inverse,
):
    count = pieces.shape[0]
    rows_own = level2_inverse.shape[1]
    level_width = level2_inverse.shape[2]
    face_rows = match_south.shape[-1]
    south_table = match_south[:, 0]
    east_table = match_east[:, 0]
    row_ids = jnp.arange(face_rows, dtype=jnp.int32)
    pick_south = (south_table[:, None, :] == row_ids[None, :, None]).astype(jnp.float32)
    send_south = (south_table[:, :, None] == row_ids[None, None, :]).astype(jnp.float32)
    pick_east = (east_table[:, None, :] == row_ids[None, :, None]).astype(jnp.float32)
    send_east = (east_table[:, :, None] == row_ids[None, None, :]).astype(jnp.float32)
    stiff_vals = stiffness.astype(jnp.float32)
    padded = jnp.pad(stiff_vals, 1)
    ratios = jnp.stack(
        [
            stiff_vals / (stiff_vals + padded[:-2, 1:-1]),
            stiff_vals / (stiff_vals + padded[2:, 1:-1]),
            stiff_vals / (stiff_vals + padded[1:-1, :-2]),
            stiff_vals / (stiff_vals + padded[1:-1, 2:]),
        ],
        axis=-1,
    )
    first_row = lax.axis_index("sub") * count
    region_row = lax.axis_index("region")
    own_ratios = lax.dynamic_slice(ratios, (first_row, region_row, jnp.int32(0)), (count, 1, 4))[
        :, 0, :
    ]
    row_weight = jnp.repeat(own_ratios, B // 4, axis=-1)[:, None, :]
    inverse = local_inverse[:, 0]
    basis = primal_basis[:, 0]
    scaled = assemble(pieces[:, 0], pick_south, pick_east, send_south, send_east) * row_weight
    local_fix = jnp.einsum("skx,sxy->sky", scaled, inverse, precision=HIGH)
    coarse_in = jnp.einsum("skx,six->ski", scaled, basis, precision=HIGH)
    lookup = (
        primal_index[:, 0, :, None] == jnp.arange(level_width, dtype=jnp.int32)[None, None, :]
    ).astype(jnp.float32)
    part_two = jnp.einsum("ski,sin->kn", coarse_in, lookup, precision=HIGH)
    region_basis = level2_basis[0]
    top_part_local = jnp.einsum("kn,tn->kt", part_two, region_basis, precision=HIGH)
    summed, top_sums = lax.psum((part_two, top_part_local), "sub")
    own_two = lax.dynamic_slice_in_dim(summed, lax.axis_index("sub") * rows_own, rows_own, 1)
    two_part = jnp.dot(own_two, level2_inverse[0], precision=HIGH)
    piece = lax.all_gather(top_sums[None], "region", axis=0, tiled=True)
    flat = jnp.transpose(piece, (1, 0, 2)).reshape(piece.shape[1], piece.shape[0] * P2)
    top_fix = jnp.dot(flat, top_inverse, precision=HIGH)
    level_two = lax.psum(two_part, "sub")
    lifted = level_two + jnp.dot(top_fix, region_basis, precision=HIGH)
    spread = jnp.einsum("kn,sin->ski", lifted, lookup, precision=HIGH)
    combined = local_fix + jnp.einsum("ski,six->skx", spread, basis, precision=HIGH)
    result = assemble(combined * row_weight, pick_south, pick_east, send_south, send_east)
    return result[:, None]


def solution(mesh):
    in_specs = (
        P("sub", "region", None, None),
        P("sub", "region", None, None),
        P("sub", "region", None, None),
        P("sub", "region", None),
        P("sub", "region", None),
        P("sub", "region", None),
        P(),
        P("region", "sub", None),
        P("region", None, None),
        P(None, "region"),
    )
    out_specs = P("sub", "region", None, None)
    return jax.shard_map(
        on_device, mesh=mesh, in_specs=in_specs, out_specs=out_specs, check_vma=False
    )
```

profile of v0, /device:TPU:6, one launch (start us, length us, event | category | flops | bytes accessed | tf_op | source)
XLA Modules:
  0.0 159.2 jit_solution(6692814678649255455)
XLA Ops:
  0.0 0.8 slice.82
  0.8 1.3 collective-permute-start.1
  2.1 1.4 convolution_bitcast_fusion.3
  3.5 3.0 %collective-permute-start = (f32[1,32,128]{2,1,0:T(8,128)S(1)}, f32[1,32,128]{2,1,0:T(8,128)S(1)}, u32[]{:S(2)}, u32[]{:S(2)}) collective-permute-start(f32[1,32,128]{2,1,0:T(8,128)S(1)} %slice.79), channel_id=1, source_target_pairs={{0,32},{32,64},{64,96},{96,128},{128,160},{160,192},{192,224},{1,3... | collective-permute-start | bytes 49160 | tf_op jit(solution)/shard_map/ppermute | solution.py:18
  6.5 0.9 slice_bitcast_fusion.1
  7.4 2.7 %collective-permute-start.3 = (f32[1,8,32,128]{3,2,1,0:T(8,128)S(1)}, f32[1,8,32,128]{3,2,1,0:T(8,128)S(1)}, u32[]{:S(2)}, u32[]{:S(2)}) collective-permute-start(f32[1,8,32,128]{3,2,1,0:T(8,128)S(1)} %slice_bitcast_fusion.1), channel_id=1, source_target_pairs={{1,0},{2,1},{3,2},{4,3},{5,4},{6,5},{7,6},{8,7},{9,8},{10,9},{11,1... | collective-permute-start | bytes 393224 | tf_op jit(solution)/shard_map/ppermute | solution.py:21
  10.2 1.4 convolution_bitcast_fusion.2
  11.6 5.2 %collective-permute-start.2 = (f32[1,8,32,128]{3,2,1,0:T(8,128)S(1)}, f32[1,8,32,128]{3,2,1,0:T(8,128)S(1)}, u32[]{:S(2)}, u32[]{:S(2)}) collective-permute-start(f32[1,8,32,128]{3,2,1,0:T(8,128)S(1)} %convolution_bitcast_fusion.2), channel_id=1, source_target_pairs={{0,1},{1,2},{2,3},{3,4},{4,5},{5,6},{6,7},{7,8},{8,9},{9,10},{10,1... | collective-permute-start | bytes 393224 | tf_op jit(solution)/shard_map/ppermute | solution.py:18
  16.8 0.7 convert_element_type.3
  17.5 0.1 fusion.48
  17.6 0.1 fusion.55
  17.7 0.1 broadcast_bitcast_fusion
  17.8 0.9 slice.81
  18.7 0.0 collective-permute-done.1
  18.7 1.1 fusion.13
  19.8 0.0 collective-permute-done.3
  19.8 1.1 convolution_bitcast_fusion.1
  20.8 0.0 collective-permute-done
  20.8 0.0 collective-permute-done.2
  20.8 0.0 copy-start.2
  20.8 1.8 %fusion.17 = f32[8,32,24]{1,2,0:T(8,128)S(1)} fusion(f32[8,1,24,512]{3,2,1,0:T(8,128)} %param.12, f32[8,32,128]{2,1,0:T(8,128)S(1)} %convolution_bitcast_fusion.1, f32[8,32,128]{2,1,0:T(8,128)S(1)} %bitcast.84, f32[8,32,128]{2,1,0:T(8,128)S(1)} %fusion.13, f32[7,32,128]{2,1,0:T(8,128)S(1)} %slice.80, f32[1,32,128]{2,1,0:T(8,128)S(1)} %collective-permute-done, ...), kind=kOutput, calls=%fused_computation.26 | convolution fusion | flops 38535168 | bytes 1482752 | tf_op jit(solution)/shard_map/skx,six->ski/dot_general | solution.py:94
  22.6 0.0 copy-start.3
  22.6 1.0 convolution_bitcast_fusion.4
  23.6 25.3 %psum.21 = f32[32,384]{1,0:T(8,128)S(1)} all-reduce(f32[32,384]{1,0:T(8,128)S(1)} %convolution_bitcast_fusion.4), channel_id=1, replica_groups=mesh['sub'=8,'region'=32] {'sub'}, use_global_device_ids=true, to_apply=%region_0.1 | all-reduce | flops 12288 | bytes 98304 | tf_op jit(solution)/shard_map/psum | solution.py:101
  48.9 1.1 convolution_bitcast_fusion.5
  50.0 1.1 fusion.46
  51.2 24.0 %all-reduce.1 = (f32[32,384]{1,0:T(8,128)S(1)}, f32[1,32,60]{2,1,0:T(8,128)S(1)}) all-reduce(f32[32,384]{1,0:T(8,128)S(1)} %fusion.46, f32[1,32,60]{2,1,0:T(8,128)S(1)} %convolution_bitcast_fusion.5), channel_id=1, replica_groups=mesh['sub'=8,'region'=32] {'sub'}, use_global_device_ids=true, to_apply=%region_1.2 | all-reduce | flops 14208 | bytes 113664 | tf_op jit(solution)/shard_map/psum | solution.py:107
  75.2 52.4 %all_gather.3 = f32[32,32,60]{2,1,0:T(8,128)S(1)} all-gather(f32[1,32,60]{2,1,0:T(8,128)S(1)} %get-tuple-element.6), channel_id=1, replica_groups=mesh['sub'=8,'region'=32] {'region'}, dimensions={0}, use_global_device_ids=true | all-gather | bytes 253440 | tf_op jit(solution)/shard_map/all_gather | solution.py:104
  127.6 0.3 copy.14
  127.9 0.3 reshape.7
  128.2 0.5 fusion.61
  128.7 1.1 fusion.8
  129.8 1.0 fusion.19
  130.8 1.6 %fusion.15 = f32[8,32,512]{2,1,0:T(8,128)S(1)} fusion(f32[8,24,32]{2,1,0:T(8,128)S(1)} %fusion.19, f32[8,1,24,512]{3,2,1,0:T(8,128)} %param.12), kind=kOutput, calls=%fused_computation.24 | convolution fusion | flops 37748736 | bytes 942080 | tf_op jit(solution)/shard_map/ski,six->skx/dot_general | solution.py:110
  132.5 7.2 %fusion.5 = f32[8,32,512]{2,1,0:T(8,128)S(1)} fusion(f32[8,32,512]{2,1,0:T(8,128)S(1)} %fusion.15, f32[8,1,512,512]{3,2,1,0:T(8,128)} %param.11, f32[8,512]{1,0:T(8,128)S(1)} %broadcast_bitcast_fusion, f32[8,32,128]{2,1,0:T(8,128)S(1)} %convolution_bitcast_fusion.1, f32[8,32,128]{2,1,0:T(8,128)S(1)} %bitcast.85, f32[8,32,128]{2,1,0:T(8,128)S(1)} %fusion.13, ...), kind=kOutput, calls=%fused_computation.3 | convolution fusion | flops 806354944 | bytes 10502144 | tf_op jit(solution)/shard_map/skx,sxy->sky/dot_general | solution.py:93
  139.7 0.5 fusion.14
  140.2 1.3 collective-permute-start.5
  141.5 0.5 convolution_bitcast_fusion
  142.0 3.0 %collective-permute-start.4 = (f32[1,32,128]{2,1,0:T(8,128)S(1)}, f32[1,32,128]{2,1,0:T(8,128)S(1)}, u32[]{:S(2)}, u32[]{:S(2)}) collective-permute-start(f32[1,32,128]{2,1,0:T(8,128)S(1)} %slice.86), channel_id=1, source_target_pairs={{0,32},{32,64},{64,96},{96,128},{128,160},{160,192},{192,224},{1,3... | collective-permute-start | bytes 49160 | tf_op jit(solution)/shard_map/ppermute | solution.py:18
  145.1 3.8 %collective-permute-start.6 = (f32[1,8,32,128]{3,2,1,0:T(8,128)S(1)}, f32[1,8,32,128]{3,2,1,0:T(8,128)S(1)}, u32[]{:S(2)}, u32[]{:S(2)}) collective-permute-start(f32[1,8,32,128]{3,2,1,0:T(8,128)S(1)} %convolution_bitcast_fusion), channel_id=1, source_target_pairs={{0,1},{1,2},{2,3},{3,4},{4,5},{5,6},{6,7},{7,8},{8,9},{9,10},{10,1... | collective-permute-start | bytes 393224 | tf_op jit(solution)/shard_map/ppermute | solution.py:18
  148.8 2.1 %collective-permute-start.7 = (f32[1,8,32,128]{3,2,1,0:T(8,128)S(1)}, f32[1,8,32,128]{3,2,1,0:T(8,128)S(1)}, u32[]{:S(2)}, u32[]{:S(2)}) collective-permute-start(f32[1,8,32,128]{3,2,1,0:T(8,128)S(1)} %slice_bitcast_fusion), channel_id=1, source_target_pairs={{1,0},{2,1},{3,2},{4,3},{5,4},{6,5},{7,6},{8,7},{9,8},{10,9},{11,1... | collective-permute-start | bytes 393224 | tf_op jit(solution)/shard_map/ppermute | solution.py:21
  150.9 0.0 collective-permute-done.5
  150.9 0.4 fusion.12
  151.3 6.7 %collective-permute-done.7 = f32[1,8,32,128]{3,2,1,0:T(8,128)S(1)} collective-permute-done((f32[1,8,32,128]{3,2,1,0:T(8,128)S(1)}, f32[1,8,32,128]{3,2,1,0:T(8,128)S(1)}, u32[]{:S(2)}, u32[]{:S(2)}) %collective-permute-start.7) | collective-permute-done | bytes 131104 | tf_op jit(solution)/shard_map/ppermute | solution.py:21
  158.0 0.4 fusion.11
  158.3 0.0 collective-permute-done.4
  158.3 0.0 collective-permute-done.6
  158.4 0.9 fusion.10
  (13 shorter events, 0.1 us)
Async XLA Ops:
  0.0 128.2 %copy-start = (f32[1920,60]{0,1:T(8,128)S(1)}, f32[1920,60]{0,1:T(8,128)}, u32[]{:S(2)}) copy-start(f32[1920,60]{0,1:T(8,128)} %param.19) | copy-start | bytes 1382404
  0.0 132.5 %copy-start.1 = (f32[8,1,32,512]{3,2,1,0:T(8,128)S(1)}, f32[8,1,32,512]{3,2,1,0:T(8,128)}, u32[]{:S(2)}) copy-start(f32[8,1,32,512]{3,2,1,0:T(8,128)} %param.10) | copy-start | bytes 1572868
  0.8 17.9 %collective-permute-start.1 = (f32[1,32,128]{2,1,0:T(8,128)S(1)}, f32[1,32,128]{2,1,0:T(8,128)S(1)}, u32[]{:S(2)}, u32[]{:S(2)}) collective-permute-start(f32[1,32,128]{2,1,0:T(8,128)S(1)} %slice.82), channel_id=1, source_target_pairs={{32,0},{64,32},{96,64},{128,96},{160,128},{192,160},{224,192},{33,... | collective-permute-start | bytes 49160 | tf_op jit(solution)/shard_map/ppermute | solution.py:21
  3.5 17.3 %collective-permute-start = (f32[1,32,128]{2,1,0:T(8,128)S(1)}, f32[1,32,128]{2,1,0:T(8,128)S(1)}, u32[]{:S(2)}, u32[]{:S(2)}) collective-permute-start(f32[1,32,128]{2,1,0:T(8,128)S(1)} %slice.79), channel_id=1, source_target_pairs={{0,32},{32,64},{64,96},{96,128},{128,160},{160,192},{192,224},{1,3... | collective-permute-start | bytes 49160 | tf_op jit(solution)/shard_map/ppermute | solution.py:18
  7.4 12.3 %collective-permute-start.3 = (f32[1,8,32,128]{3,2,1,0:T(8,128)S(1)}, f32[1,8,32,128]{3,2,1,0:T(8,128)S(1)}, u32[]{:S(2)}, u32[]{:S(2)}) collective-permute-start(f32[1,8,32,128]{3,2,1,0:T(8,128)S(1)} %slice_bitcast_fusion.1), channel_id=1, source_target_pairs={{1,0},{2,1},{3,2},{4,3},{5,4},{6,5},{7,6},{8,7},{9,8},{10,9},{11,1... | collective-permute-start | bytes 393224 | tf_op jit(solution)/shard_map/ppermute | solution.py:21
  11.6 9.3 %collective-permute-start.2 = (f32[1,8,32,128]{3,2,1,0:T(8,128)S(1)}, f32[1,8,32,128]{3,2,1,0:T(8,128)S(1)}, u32[]{:S(2)}, u32[]{:S(2)}) collective-permute-start(f32[1,8,32,128]{3,2,1,0:T(8,128)S(1)} %convolution_bitcast_fusion.2), channel_id=1, source_target_pairs={{0,1},{1,2},{2,3},{3,4},{4,5},{5,6},{6,7},{7,8},{8,9},{9,10},{10,1... | collective-permute-start | bytes 393224 | tf_op jit(solution)/shard_map/ppermute | solution.py:18
  20.8 118.9 %copy-start.2 = (s32[8,1,128]{2,1,0:T(1,128)S(1)}, s32[8,1,128]{2,1,0:T(1,128)}, u32[]{:S(2)}) copy-start(s32[8,1,128]{2,1,0:T(1,128)} %param.13) | copy-start | bytes 12292
  22.6 118.9 %copy-start.3 = (s32[8,1,128]{2,1,0:T(1,128)S(1)}, s32[8,1,128]{2,1,0:T(1,128)}, u32[]{:S(2)}) copy-start(s32[8,1,128]{2,1,0:T(1,128)} %param.14) | copy-start | bytes 12292
  140.2 10.7 %collective-permute-start.5 = (f32[1,32,128]{2,1,0:T(8,128)S(1)}, f32[1,32,128]{2,1,0:T(8,128)S(1)}, u32[]{:S(2)}, u32[]{:S(2)}) collective-permute-start(f32[1,32,128]{2,1,0:T(8,128)S(1)} %slice.89), channel_id=1, source_target_pairs={{32,0},{64,32},{96,64},{128,96},{160,128},{192,160},{224,192},{33,... | collective-permute-start | bytes 49160 | tf_op jit(solution)/shard_map/ppermute | solution.py:21
  142.0 16.3 %collective-permute-start.4 = (f32[1,32,128]{2,1,0:T(8,128)S(1)}, f32[1,32,128]{2,1,0:T(8,128)S(1)}, u32[]{:S(2)}, u32[]{:S(2)}) collective-permute-start(f32[1,32,128]{2,1,0:T(8,128)S(1)} %slice.86), channel_id=1, source_target_pairs={{0,32},{32,64},{64,96},{96,128},{128,160},{160,192},{192,224},{1,3... | collective-permute-start | bytes 49160 | tf_op jit(solution)/shard_map/ppermute | solution.py:18
  145.1 13.3 %collective-permute-start.6 = (f32[1,8,32,128]{3,2,1,0:T(8,128)S(1)}, f32[1,8,32,128]{3,2,1,0:T(8,128)S(1)}, u32[]{:S(2)}, u32[]{:S(2)}) collective-permute-start(f32[1,8,32,128]{3,2,1,0:T(8,128)S(1)} %convolution_bitcast_fusion), channel_id=1, source_target_pairs={{0,1},{1,2},{2,3},{3,4},{4,5},{5,6},{6,7},{7,8},{8,9},{9,10},{10,1... | collective-permute-start | bytes 393224 | tf_op jit(solution)/shard_map/ppermute | solution.py:18
  148.8 9.1 %collective-permute-start.7 = (f32[1,8,32,128]{3,2,1,0:T(8,128)S(1)}, f32[1,8,32,128]{3,2,1,0:T(8,128)S(1)}, u32[]{:S(2)}, u32[]{:S(2)}) collective-permute-start(f32[1,8,32,128]{3,2,1,0:T(8,128)S(1)} %slice_bitcast_fusion), channel_id=1, source_target_pairs={{1,0},{2,1},{3,2},{4,3},{5,4},{6,5},{7,6},{8,7},{9,8},{10,9},{11,1... | collective-permute-start | bytes 393224 | tf_op jit(solution)/shard_map/ppermute | solution.py:21
where the time goes:
time: 160 us; the launch traced here: 159 us
  blocking collectives  102 us (64%)
  matrix products  22.9 us (14%)
  starting transfers between devices  22.4 us (14%)
  waiting for transfers between devices  6.7 us (4%)
  local copies, waits for them, and re-layouts  3.4 us (2%)
  other arithmetic  1.78 us (1%)
    all_gather x1, blocking collectives, on_device(): piece = lax.all_gather(top_sums[None], 'region', axis=0, tiled=True)  52.4 us
    psum x1, blocking collectives, on_device(): summed, top_sums = lax.psum((part_two, top_part_local), 'sub')  25.3 us
    psum x1, blocking collectives, on_device(): level_two = lax.psum(two_part, 'sub')  24 us
    ppermute x4, starting transfers between devices, padded_2(): lax.ppermute(lax.slice_in_dim(block, block.shape[dim] - width, None, axis...  15 us
    ppermute x4, starting transfers between devices, padded_2(): lax.ppermute(lax.slice_in_dim(block, 0, width, axis=dim), axis, backward)  7.38 us
    dot_general x1, matrix products, on_device(): local_fix = jnp.einsum('skx,sxy->sky', scaled, inverse, precision=HIGH)  7.2 us
    ppermute x4, waiting for transfers between devices, padded_2(): lax.ppermute(lax.slice_in_dim(block, 0, width, axis=dim), axis, backward)  6.69 us
    dot_general x8, matrix products, permute_rows(): return jnp.einsum('skx,sxj->skj', values, table, precision=HIGH)  6.49 us
  transfers between devices with their start and end apart: 8, of which 1 were waited for; matrix products, arithmetic and copies ran while one was open for 6% of the time, Pallas kernels for 0%

commit v1 on v0

v1 whole, which is shorter than its diff:
```python
import functools

import jax
import jax.numpy as jnp
from jax import lax
from jax.experimental import pallas as pl
from jax.experimental.pallas import tpu as pltpu
from jax.sharding import PartitionSpec as P

H = 128
MESH = pl.DeviceIdType.MESH
F32 = jnp.float32
BF16 = jnp.bfloat16


def split(x):
    high = x.astype(BF16)
    return high, (x - high.astype(F32)).astype(BF16)


def nn(a, b):
    return jnp.dot(a, b, preferred_element_type=F32)


def nt(a, b):
    return lax.dot_general(a, b, (((1,), (1,)), ((), ())), preferred_element_type=F32)


def three(product, x, high, low):
    rows = x.shape[0]
    x_high, x_low = split(x)
    both = product(jnp.concatenate([x_high, x_low], axis=0), high)
    return both[:rows] + both[rows:] + product(x_high, low)


def pick(face, order):
    return jnp.take_along_axis(face, jnp.broadcast_to(order, face.shape), axis=1)


def kernel(
    S, R, NL, K, C1, P2, N2,
    pieces, local_inverse, basis, match_south, match_east, primal_index, stiffness,
    level2_inverse, level2_basis, top_inverse,
    out,
    pc, inv, bas, south, east, index, stiff, l2inv, l2b, l2pad, topv,
    colpad, weight, unsouth, uneast,
    look, lbb_high, lbb_low, lb_stack, t_high, t_low, inv_high, inv_low,
    sent_south, sent_east, got_west, got_east, got_north, got_south,
    asm, fixed, part, part_got, rows_sent, rows_got, lift_own, lift_got,
    top_sent, top_got, cast_own, cast_got, lhs, fix_own, fix_got, two, tf,
    comb, sent_south2, sent_east2, got_west2, got_east2, got_north2, got_south2,
    load_sem, edge_send, edge_recv, small_send, small_recv, step_send, step_recv,
):
    s = lax.axis_index("sub")
    b = lax.axis_index("region")
    G = K // S
    OWN = N2 // S
    north_of, south_of = (lax.rem(s + S - 1, S), b), (lax.rem(s + 1, S), b)
    west_of, east_of = (s, lax.rem(b + R - 1, R)), (s, lax.rem(b + 1, R))

    barrier = pltpu.get_barrier_semaphore()

    def tell_region(i, c):
        pl.semaphore_signal(barrier, inc=1, device_id=(s, lax.rem(b + i, R)), device_id_type=MESH)
        return c

    def tell_sub(i, c):
        pl.semaphore_signal(barrier, inc=1, device_id=(lax.rem(s + i, S), b), device_id_type=MESH)
        return c

    lax.fori_loop(1, R, tell_region, 0)
    lax.fori_loop(1, S, tell_sub, 0)

    l2inv[...] = jnp.zeros_like(l2inv)
    topv[R * P2:, :] = jnp.zeros_like(topv[R * P2:, :])
    loads = [
        pltpu.make_async_copy(match_east.at[:, 0], east, load_sem.at[0]),
        pltpu.make_async_copy(match_south.at[:, 0], south, load_sem.at[1]),
        pltpu.make_async_copy(pieces.at[:, 0], pc, load_sem.at[2]),
        pltpu.make_async_copy(stiffness, stiff, load_sem.at[3]),
        pltpu.make_async_copy(primal_index.at[:, 0], index, load_sem.at[4]),
        pltpu.make_async_copy(basis.at[:, 0], bas, load_sem.at[5]),
        pltpu.make_async_copy(level2_basis.at[0], l2b, load_sem.at[6]),
        pltpu.make_async_copy(level2_inverse.at[0], l2inv.at[pl.ds(0, OWN)], load_sem.at[7]),
        pltpu.make_async_copy(top_inverse, topv.at[pl.ds(0, R * P2)], load_sem.at[8]),
        pltpu.make_async_copy(local_inverse.at[:, 0], inv, load_sem.at[9]),
    ]
    for load in loads:
        load.start()

    lane = lax.broadcasted_iota(jnp.int32, (K, H), 1).astype(F32).astype(BF16)
    face_row = lax.broadcasted_iota(jnp.int32, (H, H), 0)

    def invert(order):
        hit = (face_row == order).astype(F32).astype(BF16)
        return nt(lane, hit).astype(jnp.int32)

    loads[0].wait()
    for a in range(NL):
        uneast[a] = invert(east[a:a + 1, :])
    loads[1].wait()
    for a in range(NL):
        unsouth[a] = invert(south[a:a + 1, :])
    loads[2].wait()
    for a in range(NL):
        sent_east[a] = pick(pc[a, :, 3 * H:], uneast[a])
    sent_south[...] = pick(pc[NL - 1, :, H:2 * H], unsouth[NL - 1])

    pl.semaphore_wait(barrier, R - 1 + S - 1)

    def remote(src, dst, send, recv, device):
        return pltpu.make_async_remote_copy(
            src_ref=src, dst_ref=dst, send_sem=send, recv_sem=recv, device_id=device,
            device_id_type=MESH)

    def edges(phase, values, east_buf, south_buf, west_got, east_got, north_got, south_got):
        def to_west(a):
            return remote(values.at[a, :, pl.ds(2 * H, H)], east_got.at[a],
                          edge_send.at[phase, 0, a], edge_recv.at[phase, 0, a], west_of)

        def to_east(a):
            return remote(east_buf.at[a], west_got.at[a],
                          edge_send.at[phase, 1, a], edge_recv.at[phase, 1, a], east_of)

        to_north = remote(values.at[0, :, pl.ds(0, H)], south_got,
                          small_send.at[phase, 0], small_recv.at[phase, 0], north_of)
        to_south = remote(south_buf, north_got,
                          small_send.at[phase, 1], small_recv.at[phase, 1], south_of)
        return to_west, to_east, to_north, to_south

    to_west, to_east, to_north, to_south = edges(
        0, pc, sent_east, sent_south, got_west, got_east, got_north, got_south)
    for a in range(NL):
        to_west(a).start()
        to_east(a).start()
    to_north.start()
    to_south.start()

    loads[3].wait()
    levels = stiff[...].astype(F32)
    place = lax.broadcasted_iota(jnp.int32, levels.shape, 1)

    def column(position):
        return jnp.sum(jnp.where(place == position, levels, 0.0), axis=1, keepdims=True)

    total = levels.shape[0]
    colpad[...] = jnp.zeros_like(colpad)
    for at, position in enumerate((b, b - 1, b + 1)):
        colpad[at, 8:8 + total, :] = jnp.broadcast_to(column(position), (total, H))
    near = colpad[0, pl.ds(pl.multiple_of(s * NL, NL), NL + 16), :]
    own = near[8:8 + NL]
    start = pl.multiple_of(s * NL + 8, 8)
    weight[:, 0:H] = own / (own + near[7:7 + NL])
    weight[:, H:2 * H] = own / (own + near[9:9 + NL])
    weight[:, 2 * H:3 * H] = own / (own + colpad[1, pl.ds(start, NL), :])
    weight[:, 3 * H:] = own / (own + colpad[2, pl.ds(start, NL), :])

    loads[4].wait()
    loads[5].wait()
    loads[6].wait()
    l2pad[...] = jnp.zeros_like(l2pad)
    l2pad[0:P2, :] = l2b[...]
    l2_high, l2_low = split(l2pad[...])
    lb_stack[0:64, :] = l2_high
    lb_stack[64:128, :] = l2_low
    unknown = lax.broadcasted_iota(jnp.int32, (N2, C1), 0)
    odd = lax.rem(b, 2)
    lbb_high[...] = jnp.zeros_like(lbb_high)
    lbb_low[...] = jnp.zeros_like(lbb_low)
    half = pl.ds(pl.multiple_of(odd * 64, 64), 64)
    for a in range(NL):
        hit = (unknown == index[a:a + 1, :]).astype(F32).astype(BF16)
        look[a] = hit
        lb = nn(lb_stack[...], hit)
        lb_high, lb_low = lb[:64].astype(BF16), lb[64:].astype(BF16)
        b_high, b_low = split(bas[a])
        both = nn(jnp.concatenate([lb_high, lb_low], axis=0), b_high)
        lbb = (both[:64] + both[64:] + nn(lb_high, b_low)) * weight[a:a + 1, :]
        high, low = split(lbb)
        lbb_high[half, 4 * H * a:4 * H * (a + 1)] = high
        lbb_low[half, 4 * H * a:4 * H * (a + 1)] = low

    loads[8].wait()

    def spread_top(p, c):
        block = topv[pl.ds(pl.multiple_of(2 * P2 * p, 8), 2 * P2 + 8), :]
        pair = jnp.concatenate([block[0:64], block[P2:P2 + 64]], axis=0)
        high, low = split(pair)
        at = pl.ds(pl.multiple_of(128 * p, 128), 128)
        t_high[at, :] = high
        t_low[at, :] = low
        return c

    lax.fori_loop(0, R // 2, spread_top, 0)

    def masked(condition, value):
        return jnp.where(condition, value, jnp.zeros_like(value))

    to_north.wait_recv()
    to_south.wait_recv()
    for a in range(NL):
        before = masked(s > 0, got_north[...]) if a == 0 else pick(
            pc[a - 1, :, H:2 * H], unsouth[a - 1])
        after = pick(masked(s < S - 1, got_south[...]) if a == NL - 1 else pc[a + 1, :, 0:H],
                     south[a:a + 1, :])
        at = 4 * H * a
        asm[:, at:at + H] = pc[a, :, 0:H] + before
        asm[:, at + H:at + 2 * H] = pc[a, :, H:2 * H] + after
    for a in range(NL):
        at = 4 * H * a
        to_east(a).wait_recv()
        asm[:, at + 2 * H:at + 3 * H] = pc[a, :, 2 * H:3 * H] + masked(b > 0, got_west[a])
        to_west(a).wait_recv()
        asm[:, at + 3 * H:at + 4 * H] = pc[a, :, 3 * H:] + masked(
            b < R - 1, pick(got_east[a], east[a:a + 1, :]))

    top = three(nt, asm[...], lbb_high[...], lbb_low[...])
    for g in range(S):
        top_sent[g] = top[G * g:G * (g + 1)]

    def others(count, me, make):
        def body(i, c):
            make(lax.rem(me + i, count)).start()
            return c
        lax.fori_loop(1, count, body, 0)

    def arrived(ref, count, sem):
        pltpu.make_async_copy(ref.at[pl.ds(0, count)], ref.at[pl.ds(0, count)], sem).wait()

    top_got[s] = top_sent[s]
    others(S, s, lambda o: remote(
        top_sent.at[o], top_got.at[s], step_send.at[0], step_recv.at[0], (o, b)))

    two_in = jnp.zeros((K, N2), F32)
    for a in range(NL):
        scaled = asm[:, 4 * H * a:4 * H * (a + 1)] * weight[a:a + 1, :]
        asm[:, 4 * H * a:4 * H * (a + 1)] = scaled
        b_high, b_low = split(bas[a])
        c_high, c_low = split(three(nt, scaled, b_high, b_low))
        both = nt(jnp.concatenate([c_high, c_low], axis=0), look[a])
        two_in += both[:K] + both[K:]
    for g in range(S):
        turned = two_in if g == 0 else pltpu.roll(two_in, N2 - OWN * g, 1)
        part[g] = turned[:, 0:H]
    part_got[s] = part[s]
    others(S, s, lambda o: remote(
        part.at[o], part_got.at[s], step_send.at[1], step_recv.at[1], (o, b)))

    arrived(top_got, S - 1, step_recv.at[0])
    mine = top_got[0]
    for g in range(1, S):
        mine += top_got[g]
    cast_own[...] = mine
    cast_got[b] = mine

    def cast(i, c):
        o = lax.rem(b + R // 2 + i, R)

        remote(cast_own, cast_got.at[b], step_send.at[2], step_recv.at[2], (s, o)).start()
        return c

    lax.fori_loop(0, R // 2, cast, 0)
    lax.fori_loop(R // 2 + 1, R, cast, 0)

    loads[9].wait()

    def solve(a, c):
        high, low = split(inv[a])
        at = pl.ds(pl.multiple_of(4 * H * a, 4 * H), 4 * H)
        fixed[:, at] = three(nn, asm[:, at], high, low)
        return c

    lax.fori_loop(0, NL // 2, solve, 0)

    loads[7].wait()
    arrived(part_got, S - 1, step_recv.at[1])
    own_two = part_got[0]
    for g in range(1, S):
        own_two += part_got[g]
    i_high, i_low = split(l2inv[...])
    lift = three(nn, own_two, i_high, i_low)
    for g in range(S):
        rows_sent[g] = lift[G * g:G * (g + 1)]
    rows_got[s] = rows_sent[s]
    others(S, s, lambda o: remote(
        rows_sent.at[o], rows_got.at[s], step_send.at[3], step_recv.at[3], (o, b)))
    lax.fori_loop(NL // 2, NL, solve, 0)
    arrived(rows_got, S - 1, step_recv.at[3])
    lift4 = rows_got[0]
    for g in range(1, S):
        lift4 += rows_got[g]
    lift_own[...] = lift4
    lift_got[s] = lift4
    others(S, s, lambda o: remote(
        lift_own, lift_got.at[s], step_send.at[4], step_recv.at[4], (o, b)))

    arrived(cast_got, R - 1, step_recv.at[2])
    for p in range(R // 2):
        pair = cast_got[2 * p] + cast_got[2 * p + 1]
        high = pair.astype(BF16).astype(F32)
        lhs[0:G, H * p:H * (p + 1)] = high
        lhs[G:2 * G, H * p:H * (p + 1)] = pair - high
    left = lhs[...].astype(BF16)
    first = nn(left, t_high[...])
    fix = first[0:G] + first[G:2 * G] + nn(left, t_low[...])[0:G]
    fix_own[...] = jnp.zeros_like(fix_own)
    fix_own[:, 0:P2] = fix
    fix = fix_own[...]
    fix = jnp.where(odd == 1, pltpu.roll(fix, 64, 1), fix)
    fix_own[...] = fix
    fix_got[s] = fix
    others(S, s, lambda o: remote(
        fix_own, fix_got.at[s], step_send.at[5], step_recv.at[5], (o, b)))

    arrived(lift_got, S - 1, step_recv.at[4])
    for g in range(S):
        two[G * g:G * (g + 1), :] = lift_got[g]
    two_high, two_low = split(two[...])
    two_both = jnp.concatenate([two_high, two_low], axis=0)
    for a in range(NL):
        e = nn(two_both, look[a])
        b_high, b_low = split(bas[a])
        at = 4 * H * a
        fixed[:, at:at + 4 * H] = (fixed[:, at:at + 4 * H] + three(
            nn, e[:K] + e[K:], b_high, b_low)) * weight[a:a + 1, :]

    arrived(fix_got, S - 1, step_recv.at[5])
    for g in range(S):
        tf[G * g:G * (g + 1), :] = fix_got[g]
    f_high, f_low = split(tf[...])
    f_both = jnp.concatenate([f_high, f_low], axis=0)

    to_west2, to_east2, to_north2, to_south2 = edges(
        1, comb, sent_east2, sent_south2, got_west2, got_east2, got_north2, got_south2)
    for a in range(NL):
        at = 4 * H * a
        both = nn(f_both, lbb_high[:, at:at + 4 * H])
        value = fixed[:, at:at + 4 * H] + both[:K] + both[K:] + nn(
            f_high, lbb_low[:, at:at + 4 * H])
        comb[a] = value
        to_west2(a).start()
        sent_east2[a] = pick(value[:, 3 * H:], uneast[a])
        to_east2(a).start()
        if a == 0:
            to_north2.start()
        if a == NL - 1:
            sent_south2[...] = pick(value[:, H:2 * H], unsouth[a])
            to_south2.start()

    to_north2.wait_recv()
    to_south2.wait_recv()
    for a in range(NL):
        before = masked(s > 0, got_north2[...]) if a == 0 else pick(
            comb[a - 1, :, H:2 * H], unsouth[a - 1])
        after = pick(masked(s < S - 1, got_south2[...]) if a == NL - 1 else comb[a + 1, :, 0:H],
                     south[a:a + 1, :])
        out[a, 0, :, 0:H] = comb[a, :, 0:H] + before
        out[a, 0, :, H:2 * H] = comb[a, :, H:2 * H] + after
    for a in range(NL):
        to_east2(a).wait_recv()
        out[a, 0, :, 2 * H:3 * H] = comb[a, :, 2 * H:3 * H] + masked(b > 0, got_west2[a])
        to_west2(a).wait_recv()
        out[a, 0, :, 3 * H:] = comb[a, :, 3 * H:] + masked(
            b < R - 1, pick(got_east2[a], east[a:a + 1, :]))

    for first in ((to_west, to_east, to_north, to_south),
                  (to_west2, to_east2, to_north2, to_south2)):
        for a in range(NL):
            first[0](a).wait_send()
            first[1](a).wait_send()
        first[2].wait_send()
        first[3].wait_send()
    arrived(top_got, S - 1, step_send.at[0])
    arrived(part_got, S - 1, step_send.at[1])
    arrived(cast_got, R - 1, step_send.at[2])
    arrived(rows_got, S - 1, step_send.at[3])
    arrived(lift_got, S - 1, step_send.at[4])
    arrived(fix_got, S - 1, step_send.at[5])


def solution(mesh):
    S, R = mesh.shape["sub"], mesh.shape["region"]

    def on_device(*args):
        NL, _, K, B = args[0].shape
        C1 = args[2].shape[2]
        P2, N2 = args[8].shape[1:]
        NA = args[6].shape[0]
        G = K // S
        vm = pltpu.VMEM
        edge = [
            vm((K, H), F32), vm((NL, K, H), F32), vm((NL, K, H), F32), vm((NL, K, H), F32),
            vm((K, H), F32), vm((K, H), F32)]
        scratch = [
            vm((NL, K, B), F32), vm((NL, B, B), F32), vm((NL, C1, B), F32),
            vm((NL, H), jnp.int32), vm((NL, H), jnp.int32), vm((NL, C1), jnp.int32),
            vm(args[6].shape, jnp.int32), vm((H, N2), F32), vm((P2, N2), F32), vm((64, N2), F32),
            vm((R * P2 + 8, P2), F32),
            vm((3, NA + 16, H), F32), vm((NL, B), F32),
            vm((NL, K, H), jnp.int32), vm((NL, K, H), jnp.int32),
            vm((NL, N2, C1), BF16), vm((128, NL * B), BF16), vm((128, NL * B), BF16),
            vm((128, N2), BF16), vm((64 * R, P2), BF16), vm((64 * R, P2), BF16),
            vm((16, 128), BF16), vm((16, 128), BF16),
            *edge,
            vm((K, NL * B), F32), vm((K, NL * B), F32),
            vm((S, K, H), F32), vm((S, K, H), F32),
            vm((S, G, N2), F32), vm((S, G, N2), F32), vm((G, N2), F32), vm((S, G, N2), F32),
            vm((S, G, H), F32), vm((S, G, H), F32), vm((G, H), F32), vm((R, G, H), F32),
            vm((2 * G, R // 2 * H), F32), vm((G, H), F32), vm((S, G, H), F32),
            vm((K, N2), F32), vm((K, H), F32),
            vm((NL, K, B), F32), *edge,
            pltpu.SemaphoreType.DMA((10,)),
            pltpu.SemaphoreType.DMA((2, 2, NL)), pltpu.SemaphoreType.DMA((2, 2, NL)),
            pltpu.SemaphoreType.DMA((2, 2)), pltpu.SemaphoreType.DMA((2, 2)),
            pltpu.SemaphoreType.DMA((6,)), pltpu.SemaphoreType.DMA((6,)),
        ]
        return pl.pallas_call(
            functools.partial(kernel, S, R, NL, K, C1, P2, N2),
            out_shape=jax.ShapeDtypeStruct(args[0].shape, F32),
            in_specs=[pl.BlockSpec(memory_space=pl.ANY)] * len(args),
            out_specs=pl.BlockSpec(memory_space=pltpu.VMEM),
            scratch_shapes=scratch,
            compiler_params=pltpu.CompilerParams(
                collective_id=0, has_side_effects=True, vmem_limit_bytes=56 * 2**20),
        )(*args)

    in_specs = (
        P("sub", "region", None, None),
        P("sub", "region", None, None),
        P("sub", "region", None, None),
        P("sub", "region", None),
        P("sub", "region", None),
        P("sub", "region", None),
        P(),
        P("region", "sub", None),
        P("region", None, None),
        P(None, "region"),
    )
    out_specs = P("sub", "region", None, None)
    return jax.shard_map(
        on_device, mesh=mesh, in_specs=in_specs, out_specs=out_specs, check_vma=False
    )
```

time: 160 us -> 49.4 us (0.31)
  the two profiles are of different devices: /device:TPU:6 before, /device:TPU:1 now
where the time goes in v1:
time: 49.4 us; the launch traced here: 49.1 us
  Pallas kernels  42 us (85%)
  local copies, waits for them, and re-layouts  7.14 us (14%)
    pallas_call x1, Pallas kernels, on_device(): pl.pallas_call(functools.partial(kernel, S, R, NL, K, C1, P2, N2), out_sh...  42 us
    unnamed x4, local copies, waits for them, and re-layouts  7.14 us

profile of v1, /device:TPU:1, one launch (start us, length us, event | category | flops | bytes accessed | tf_op | source)
XLA Modules:
  0.0 49.1 jit_solution(6161820562231393319)
XLA Ops:
  0.0 1.4 %copy.11.stiffness = s32[64,32]{1,0:T(8,128)} copy(s32[64,32]{0,1:T(8,128)} %param.16) | data formatting | bytes 16384 | tf_op args[6]
  1.4 1.5 %copy.12.level2_basis = f32[1,60,384]{2,1,0:T(8,128)} copy(f32[1,60,384]{2,0,1:T(1,128)} %param.18) | data formatting | bytes 184320 | tf_op args[8]
  2.9 2.3 %copy.13.top_inverse = f32[1920,60]{1,0:T(8,128)} copy(f32[1920,60]{0,1:T(8,128)} %param.19) | data formatting | bytes 921600 | tf_op args[9]
  5.3 42.0 %shard_map.100 = f32[8,1,32,512]{3,2,1,0:T(8,128)} custom-call(f32[8,1,32,512]{3,2,1,0:T(8,128)} %pieces.1, f32[8,1,512,512]{3,2,1,0:T(8,128)} %local_inverse.1, f32[8,1,24,512]{3,2,1,0:T(8,128)} %basis.1, s32[8,1,128]{2,1,0:T(1,128)} %match_south.1, s32[8,1,128]{2,1,0:T(1,128)} %match_east.1, s32[8,1,24]{2,1,0:T(1,128)} %primal_index.1, ...), custom_call_target="tpu_custom_call" | custom-call | tf_op jit(solution)/shard_map/pallas_call | solution.py:417
  47.3 1.9 %copy.15 = f32[8,1,32,512]{3,2,1,0:T(8,128)} copy(f32[8,1,32,512]{3,2,1,0:T(8,128)} %shard_map.100) | data formatting | bytes 1048576

commit v2 on v1

v2 whole, which is shorter than its diff:
```python
import functools

import jax
import jax.numpy as jnp
from jax import lax
from jax.experimental import pallas as pl
from jax.experimental.pallas import tpu as pltpu
from jax.sharding import PartitionSpec as P

H = 128
EARLY = 4
MESH = pl.DeviceIdType.MESH
F32 = jnp.float32
BF16 = jnp.bfloat16


def split(x):
    high = x.astype(BF16)
    return high, (x - high.astype(F32)).astype(BF16)


def nn(a, b):
    return jnp.dot(a, b, preferred_element_type=F32)


def nt(a, b):
    return lax.dot_general(a, b, (((1,), (1,)), ((), ())), preferred_element_type=F32)


def three(product, x, high, low):
    rows = x.shape[0]
    x_high, x_low = split(x)
    both = product(jnp.concatenate([x_high, x_low], axis=0), high)
    return both[:rows] + both[rows:] + product(x_high, low)


def pick(face, order):
    return jnp.take_along_axis(face, jnp.broadcast_to(order, face.shape), axis=1)


def kernel(
    S, R, NL, K, C1, P2, N2,
    pieces, local_inverse, basis, match_south, match_east, primal_index, stiffness,
    level2_inverse, level2_basis, top_inverse,
    out,
    pc, inv, bas, south, east, north_table, west_table, index, stiff, l2inv, l2b, l2pad, topt, topv,
    weight, unsouth, unwest,
    look, lbb_high, lbb_low, lb_stack, t_high, t_low,
    got_west, got_east, got_north, got_south,
    asm, fixed, lhs_two, rows_sent, rows_got, lift_own, lift_got,
    top_sent, top_got, cast_own, cast_got, lhs, fix_own, fix_got, two, tf,
    comb, got_west2, got_east2, got_north2, got_south2,
    weight_near, bas_west, bas_east, bas_north, bas_south, index_west, index_east, index_north,
    index_south, l2_west, l2_east, slots, looks, big_b_high, big_b_low, big_q_high, big_q_low,
    fix_rolled, more_send, more_recv,
    load_sem, edge_send, edge_recv, small_send, small_recv, step_send, step_recv,
):
    s = lax.axis_index("sub")
    b = lax.axis_index("region")
    G = K // S
    OWN = N2 // S
    north_of, south_of = (lax.rem(s + S - 1, S), b), (lax.rem(s + 1, S), b)
    west_of, east_of = (s, lax.rem(b + R - 1, R)), (s, lax.rem(b + 1, R))

    barrier = pltpu.get_barrier_semaphore()

    def tell_region(i, c):
        pl.semaphore_signal(barrier, inc=1, device_id=(s, lax.rem(b + i, R)), device_id_type=MESH)
        return c

    def tell_sub(i, c):
        for region in (b, east_of[1], west_of[1]):
            pl.semaphore_signal(
                barrier, inc=1, device_id=(lax.rem(s + i, S), region), device_id_type=MESH)
        return c

    own_rows = pl.ds(pl.multiple_of(s * OWN, 8), OWN)
    loads = [
        pltpu.make_async_copy(match_east.at[:, 0], east, load_sem.at[0]),
        pltpu.make_async_copy(match_south.at[:, 0], south, load_sem.at[1]),
        pltpu.make_async_copy(pieces.at[:, 0], pc, load_sem.at[2]),
        pltpu.make_async_copy(stiffness, stiff, load_sem.at[3]),
        pltpu.make_async_copy(primal_index.at[:, 0], index, load_sem.at[4]),
        pltpu.make_async_copy(basis.at[:, 0], bas, load_sem.at[5]),
        pltpu.make_async_copy(level2_basis.at[:, 0], l2b, load_sem.at[6]),
        pltpu.make_async_copy(level2_inverse.at[0], l2inv.at[own_rows], load_sem.at[7]),
        pltpu.make_async_copy(top_inverse, topt, load_sem.at[8]),
        pltpu.make_async_copy(local_inverse.at[:, 0], inv, load_sem.at[9]),
    ]
    lax.fori_loop(1, R, tell_region, 0)
    lax.fori_loop(1, S, tell_sub, 0)
    for load in loads:
        load.start()
    pl.semaphore_wait(barrier, R - 1 + 3 * (S - 1))

    def remote(src, dst, send, recv, device):
        return pltpu.make_async_remote_copy(
            src_ref=src, dst_ref=dst, send_sem=send, recv_sem=recv, device_id=device,
            device_id_type=MESH)

    def edges(phase, face, west_got, east_got, north_got, south_got):
        def to_west(a):
            return remote(face(a, 2), east_got.at[a],
                          edge_send.at[phase, 0, a], edge_recv.at[phase, 0, a], west_of)

        def to_east(a):
            return remote(face(a, 3), west_got.at[a],
                          edge_send.at[phase, 1, a], edge_recv.at[phase, 1, a], east_of)

        to_north = remote(face(0, 0), south_got,
                          small_send.at[phase, 0], small_recv.at[phase, 0], north_of)
        to_south = remote(face(NL - 1, 1), north_got,
                          small_send.at[phase, 1], small_recv.at[phase, 1], south_of)
        return to_west, to_east, to_north, to_south

    to_west, to_east, to_north, to_south = edges(
        0, lambda a, f: pieces.at[a, 0, :, pl.ds(f * H, H)],
        got_west, got_east, got_north, got_south)
    table_east = remote(match_east.at[:, 0], west_table,
                        small_send.at[0, 2], small_recv.at[0, 2], east_of)
    table_south = remote(match_south.at[NL - 1], north_table,
                         small_send.at[0, 3], small_recv.at[0, 3], south_of)
    table_east.start()
    table_south.start()
    for a in range(NL):
        to_west(a).start()
        to_east(a).start()
    to_north.start()
    to_south.start()

    def others(count, me, make):
        def body(i, c):
            make(lax.rem(me + i, count)).start()
            return c
        lax.fori_loop(1, count, body, 0)

    others(S, s, lambda o: remote(
        level2_inverse.at[0], l2inv.at[own_rows], step_send.at[3], step_recv.at[3], (o, b)))

    def face(f):
        return basis.at[:, 0, :, pl.ds(f * H, H)]

    more = [(face(3), bas_west, east_of), (primal_index.at[:, 0], index_west, east_of),
            (level2_basis.at[:, 0], l2_west, east_of),
            (face(2), bas_east, west_of), (primal_index.at[:, 0], index_east, west_of),
            (level2_basis.at[:, 0], l2_east, west_of),
            (basis.at[NL - 1, 0, :, pl.ds(H, H)], bas_north, south_of),
            (primal_index.at[NL - 1], index_north, south_of),
            (basis.at[0, 0, :, pl.ds(0, H)], bas_south, north_of),
            (primal_index.at[0], index_south, north_of)]
    more = [remote(src, dst, more_send.at[i], more_recv.at[i], device)
            for i, (src, dst, device) in enumerate(more)]
    for copy in more:
        copy.start()

    lane = lax.broadcasted_iota(jnp.int32, (K, H), 1).astype(F32).astype(BF16)
    face_row = lax.broadcasted_iota(jnp.int32, (H, H), 0)

    def invert(order):
        hit = (face_row == order).astype(F32).astype(BF16)
        return nt(lane, hit).astype(jnp.int32)

    loads[0].wait()
    loads[1].wait()
    for a in range(NL - 1):
        unsouth[a] = invert(south[a:a + 1, :])

    loads[3].wait()
    levels = stiff[...].astype(F32)
    regions = lax.broadcasted_iota(jnp.int32, levels.shape, 0)
    spots = (lax.broadcasted_iota(jnp.int32, (NL, levels.shape[1]), 1)
             - lax.broadcasted_iota(jnp.int32, (NL, levels.shape[1]), 0) - s * NL)

    def level(region, step):
        row = jnp.sum(jnp.where(regions == region, levels, 0.0), axis=0, keepdims=True)
        return jnp.sum(jnp.where(spots == step, row, 0.0), axis=1, keepdims=True)

    own = level(b, 0)
    for f, other in enumerate((level(b, -1), level(b, 1), level(b - 1, 0), level(b + 1, 0))):
        weight[:, f * H:(f + 1) * H] = jnp.broadcast_to(own / (own + other), (NL, H))
        weight_near[:, f * H:(f + 1) * H] = jnp.broadcast_to(other / (own + other), (NL, H))

    loads[4].wait()
    loads[5].wait()
    loads[6].wait()
    l2pad[...] = jnp.zeros_like(l2pad)
    l2pad[0:P2, :] = l2b[...]
    l2_high, l2_low = split(l2pad[...])
    lb_stack[0:64, :] = l2_high
    lb_stack[64:128, :] = l2_low
    unknown = lax.broadcasted_iota(jnp.int32, (N2, C1), 0)
    odd = lax.rem(b, 2)
    lbb_high[...] = jnp.zeros_like(lbb_high)
    lbb_low[...] = jnp.zeros_like(lbb_low)
    half = pl.ds(pl.multiple_of(odd * 64, 64), 64)
    for a in range(NL):
        hit = (unknown == index[a:a + 1, :]).astype(F32).astype(BF16)
        look[a] = hit
        lb = nn(lb_stack[...], hit)
        lb_high, lb_low = lb[:64].astype(BF16), lb[64:].astype(BF16)
        b_high, b_low = split(bas[a])
        both = nn(jnp.concatenate([lb_high, lb_low], axis=0), b_high)
        lbb = (both[:64] + both[64:] + nn(lb_high, b_low)) * weight[a:a + 1, :]
        high, low = split(lbb)
        lbb_high[half, 4 * H * a:4 * H * (a + 1)] = high
        lbb_low[half, 4 * H * a:4 * H * (a + 1)] = low

    loads[8].wait()
    for c in range(R * P2 // 128):
        topv[128 * c:128 * (c + 1), :] = topt[:, 128 * c:128 * (c + 1)].T
    topv[R * P2:, :] = jnp.zeros_like(topv[R * P2:, :])

    def spread_top(p, c):
        block = topv[pl.ds(pl.multiple_of(2 * P2 * p, 8), 2 * P2 + 8), :]
        pair = jnp.concatenate([block[0:64], block[P2:P2 + 64]], axis=0)
        high, low = split(pair)
        at = pl.ds(pl.multiple_of(128 * p, 128), 128)
        t_high[at, :] = high
        t_low[at, :] = low
        return c

    lax.fori_loop(0, R // 2, spread_top, 0)

    def masked(condition, value):
        return jnp.where(condition, value, jnp.zeros_like(value))

    table_south.wait_recv()
    unsouth[NL - 1] = invert(north_table[...])
    table_east.wait_recv()
    for a in range(NL):
        unwest[a] = invert(west_table[a:a + 1, :])
    loads[2].wait()
    to_north.wait_recv()
    to_south.wait_recv()
    for a in range(NL):
        before = pick(masked(s > 0, got_north[...]) if a == 0 else pc[a - 1, :, H:2 * H],
                      unsouth[(a + NL - 1) % NL])
        after = pick(masked(s < S - 1, got_south[...]) if a == NL - 1 else pc[a + 1, :, 0:H],
                     south[a:a + 1, :])
        at = 4 * H * a
        asm[:, at:at + H] = pc[a, :, 0:H] + before
        asm[:, at + H:at + 2 * H] = pc[a, :, H:2 * H] + after
    for a in range(NL):
        at = 4 * H * a
        to_east(a).wait_recv()
        asm[:, at + 2 * H:at + 3 * H] = pc[a, :, 2 * H:3 * H] + masked(
            b > 0, pick(got_west[a], unwest[a]))
        to_west(a).wait_recv()
        asm[:, at + 3 * H:at + 4 * H] = pc[a, :, 3 * H:] + masked(
            b < R - 1, pick(got_east[a], east[a:a + 1, :]))

    top = three(nt, asm[...], lbb_high[...], lbb_low[...])
    for g in range(S):
        top_sent[g] = top[G * g:G * (g + 1)]

    def arrived(ref, count, sem):
        pltpu.make_async_copy(ref.at[pl.ds(0, count)], ref.at[pl.ds(0, count)], sem).wait()

    top_got[s] = top_sent[s]
    others(S, s, lambda o: remote(
        top_sent.at[o], top_got.at[s], step_send.at[0], step_recv.at[0], (o, b)))

    two_in = jnp.zeros((K, N2), F32)
    for a in range(NL):
        scaled = asm[:, 4 * H * a:4 * H * (a + 1)] * weight[a:a + 1, :]
        asm[:, 4 * H * a:4 * H * (a + 1)] = scaled
        b_high, b_low = split(bas[a])
        c_high, c_low = split(three(nt, scaled, b_high, b_low))
        both = nt(jnp.concatenate([c_high, c_low], axis=0), look[a])
        two_in += both[:K] + both[K:]
    for g in range(S):
        rows_sent[g] = two_in[G * g:G * (g + 1)]
    rows_got[s] = rows_sent[s]
    others(S, s, lambda o: remote(
        rows_sent.at[o], rows_got.at[s], step_send.at[1], step_recv.at[1], (o, b)))

    to_west2, to_east2, to_north2, to_south2 = edges(
        1, lambda a, f: comb.at[a, :, pl.ds(f * H, H)],
        got_west2, got_east2, got_north2, got_south2)
    loads[9].wait()

    def solve(a, c):
        high, low = split(inv[a])
        at = pl.ds(pl.multiple_of(4 * H * a, 4 * H), 4 * H)
        comb[a] = three(nn, asm[:, at], high, low) * weight[pl.ds(a, 1), :]
        to_west2(a).start()
        to_east2(a).start()
        return c

    lax.fori_loop(0, EARLY, solve, 0)

    arrived(top_got, S - 1, step_recv.at[0])
    mine = top_got[0]
    for g in range(1, S):
        mine += top_got[g]
    cast_own[...] = mine
    cast_got[b] = mine

    def cast(i, c):
        o = lax.rem(b + R // 2 + i, R)

        remote(cast_own, cast_got.at[b], step_send.at[2], step_recv.at[2], (s, o)).start()
        return c

    lax.fori_loop(0, R // 2, cast, 0)
    lax.fori_loop(R // 2 + 1, R, cast, 0)

    lax.fori_loop(EARLY, NL, solve, 0)
    to_north2.start()
    to_south2.start()

    loads[7].wait()
    arrived(l2inv, (S - 1) * OWN, step_recv.at[3])
    i_high, i_low = split(l2inv[...])
    arrived(rows_got, S - 1, step_recv.at[1])
    two_mine = rows_got[0]
    for g in range(1, S):
        two_mine += rows_got[g]
    high = two_mine.astype(BF16).astype(F32)
    lhs_two[0:G, :] = high
    lhs_two[G:2 * G, :] = two_mine - high
    left = lhs_two[...].astype(BF16)
    first = nn(left, i_high)
    lift4 = first[0:G] + first[G:2 * G] + nn(left, i_low)[0:G]
    lift_own[...] = lift4
    lift_got[s] = lift4

    def spread(i, src, rolled, got, k):
        o = lax.rem(s + i, S)
        remote(rolled, got.at[S + s], step_send.at[k], step_recv.at[k], (o, east_of[1])).start()
        remote(src, got.at[2 * S + s], step_send.at[k], step_recv.at[k], (o, west_of[1])).start()

    def to_three_regions(src, rolled, got, k):
        def body(i, c):
            spread(i, src, rolled, got, k)
            o = lax.rem(s + i, S)
            remote(src, got.at[s], step_send.at[k], step_recv.at[k], (o, b)).start()
            return c
        lax.fori_loop(1, S, body, 0)
        spread(0, src, rolled, got, k)

    to_three_regions(lift_own, lift_own, lift_got, 4)

    for copy in more:
        copy.wait_recv()
    slots[...] = jnp.full_like(slots, -1)
    slots[:, 0:C1] = index[...]
    slots[0:1, C1:2 * C1] = index_north[...]
    slots[1:NL, C1:2 * C1] = index[0:NL - 1, :]
    slots[0:NL - 1, 2 * C1:3 * C1] = index[1:NL, :]
    slots[NL - 1:NL, 2 * C1:3 * C1] = index_south[...]
    slots[:, 3 * C1:4 * C1] = index_west[...]
    slots[:, 4 * C1:5 * C1] = index_east[...]
    stacks = [lb_stack[...]]
    for level2 in (l2_west, l2_east):
        l2pad[0:P2, :] = level2[...]
        stacks.append(jnp.concatenate(split(l2pad[...]), axis=0))
    spot = lax.broadcasted_iota(jnp.int32, (N2, H), 1)
    unknown = lax.broadcasted_iota(jnp.int32, (N2, H), 0)
    big_q_high[:, 192:256, :] = jnp.zeros_like(big_q_high[:, 192:256, :])
    big_q_low[:, 192:256, :] = jnp.zeros_like(big_q_low[:, 192:256, :])
    gap = jnp.zeros((C1, H), F32)
    for a in range(NL):
        hit = jnp.where(unknown == slots[a:a + 1, :], 1.0, 0.0)
        lb_high, lb_low = [], []
        for j, (low_end, high_end) in enumerate(((0, 3), (3, 4), (4, 5))):
            own_hit = jnp.where((spot >= low_end * C1) & (spot < high_end * C1), hit, 0.0).astype(BF16)
            looks[a, j * N2:(j + 1) * N2, :] = own_hit
            lb = nn(stacks[j], own_hit)
            lb_high.append(lb[0:64])
            lb_low.append(lb[64:128])
        north = bas_north[...] if a == 0 else bas[a - 1, :, H:2 * H]
        north_weight = weight_near[0:1, 0:H] if a == 0 else weight[a - 1:a, H:2 * H]
        after = bas_south[...] if a == NL - 1 else bas[a + 1, :, 0:H]
        after_weight = (weight_near[a:a + 1, H:2 * H] if a == NL - 1
                        else weight[a + 1:a + 2, 0:H])
        faces = [
            pick(north, unsouth[(a + NL - 1) % NL, 0:1, :]) * north_weight,
            pick(after, south[a:a + 1, :]) * after_weight,
            pick(bas_west[a], unwest[a, 0:1, :]) * weight_near[a:a + 1, 2 * H:3 * H],
            pick(bas_east[a], east[a:a + 1, :]) * weight_near[a:a + 1, 3 * H:]]
        rows = [bas[a] * weight[a:a + 1, :]]
        for f in range(4):
            rows.append(jnp.concatenate([gap] * f + [faces[f]] + [gap] * (3 - f), axis=1))
        rows.append(jnp.zeros((H - 5 * C1, 4 * H), F32))
        high, low = split(jnp.concatenate(rows, axis=0))
        big_b_high[a] = high
        big_b_low[a] = low
        q_high = jnp.concatenate(lb_high, axis=0).astype(BF16)
        q_low = jnp.concatenate(lb_low, axis=0).astype(BF16)
        both = nn(jnp.concatenate([q_high, q_low], axis=0), high)
        q_high, q_low = split(both[0:192] + both[192:] + nn(q_high, low))
        big_q_high[a, 0:192, :] = q_high
        big_q_low[a, 0:192, :] = q_low

    arrived(cast_got, R - 1, step_recv.at[2])
    for p in range(R // 2):
        pair = cast_got[2 * p] + cast_got[2 * p + 1]
        high = pair.astype(BF16).astype(F32)
        lhs[0:G, H * p:H * (p + 1)] = high
        lhs[G:2 * G, H * p:H * (p + 1)] = pair - high
    left = lhs[...].astype(BF16)
    first = nn(left, t_high[...])
    fix = first[0:G] + first[G:2 * G] + nn(left, t_low[...])[0:G]
    fix_own[...] = jnp.zeros_like(fix_own)
    fix_own[:, 0:P2] = fix
    fix = fix_own[...]
    fix_rolled[...] = pltpu.roll(fix, 64, 1)
    fix_got[s] = fix
    to_three_regions(fix_own, fix_rolled, fix_got, 5)

    to_north2.wait_recv()
    to_south2.wait_recv()
    for a in range(NL):
        before = pick(masked(s > 0, got_north2[...]) if a == 0 else comb[a - 1, :, H:2 * H],
                      unsouth[(a + NL - 1) % NL])
        after = pick(masked(s < S - 1, got_south2[...]) if a == NL - 1 else comb[a + 1, :, 0:H],
                     south[a:a + 1, :])
        to_east2(a).wait_recv()
        to_west2(a).wait_recv()
        west = masked(b > 0, pick(got_west2[a], unwest[a]))
        east_side = masked(b < R - 1, pick(got_east2[a], east[a:a + 1, :]))
        fixed[:, 4 * H * a:4 * H * (a + 1)] = comb[a] + jnp.concatenate(
            [before, after, west, east_side], axis=1)

    arrived(lift_got, 3 * S - 1, step_recv.at[4])
    for j in range(3):
        for g in range(S):
            two[G * g:G * (g + 1), j * N2:(j + 1) * N2] = lift_got[j * S + g]
    two_both = jnp.concatenate(split(two[...]), axis=0)
    for a in range(NL):
        e = nn(two_both, looks[a])
        at = 4 * H * a
        fixed[:, at:at + 4 * H] += three(nn, e[:K] + e[K:], big_b_high[a], big_b_low[a])

    arrived(fix_got, 3 * S - 1, step_recv.at[5])
    for g in range(S):
        tf[G * g:G * (g + 1), 0:H] = fix_got[g] + fix_got[S + g]
        tf[G * g:G * (g + 1), H:2 * H] = fix_got[2 * S + g]
    f_high, f_low = split(tf[...])
    f_both = jnp.concatenate([f_high, f_low], axis=0)
    for a in range(NL):
        both = nn(f_both, big_q_high[a])
        out[a, 0] = fixed[:, 4 * H * a:4 * H * (a + 1)] + both[:K] + both[K:] + nn(
            f_high, big_q_low[a])

    for first in ((to_west, to_east, to_north, to_south),
                  (to_west2, to_east2, to_north2, to_south2)):
        for a in range(NL):
            first[0](a).wait_send()
            first[1](a).wait_send()
        first[2].wait_send()
        first[3].wait_send()
    for copy in more:
        copy.wait_send()
    table_east.wait_send()
    table_south.wait_send()
    arrived(top_got, S - 1, step_send.at[0])
    arrived(rows_got, S - 1, step_send.at[1])
    arrived(cast_got, R - 1, step_send.at[2])
    arrived(l2inv, (S - 1) * OWN, step_send.at[3])
    arrived(lift_got, 3 * S - 1, step_send.at[4])
    arrived(fix_got, 3 * S - 1, step_send.at[5])


def solution(mesh):
    S, R = mesh.shape["sub"], mesh.shape["region"]

    def on_device(*args):
        NL, _, K, B = args[0].shape
        C1 = args[2].shape[2]
        P2, N2 = args[8].shape[1:]
        NA = args[6].shape[0]
        G = K // S
        vm = pltpu.VMEM
        edge = [vm((NL, K, H), F32), vm((NL, K, H), F32), vm((K, H), F32), vm((K, H), F32)]
        scratch = [
            vm((NL, K, B), F32), vm((NL, B, B), F32), vm((NL, C1, B), F32),
            vm((NL, H), jnp.int32), vm((NL, H), jnp.int32), vm((1, H), jnp.int32),
            vm((NL, H), jnp.int32), vm((NL, C1), jnp.int32), vm((R, NA), jnp.int32), vm((N2, N2), F32), vm((P2, N2), F32), vm((64, N2), F32),
            vm((P2, R * P2), F32), vm((R * P2 + 8, P2), F32), vm((NL, B), F32),
            vm((NL, K, H), jnp.int32), vm((NL, K, H), jnp.int32),
            vm((NL, N2, C1), BF16), vm((128, NL * B), BF16), vm((128, NL * B), BF16),
            vm((128, N2), BF16), vm((64 * R, P2), BF16), vm((64 * R, P2), BF16),
            *edge,
            vm((K, NL * B), F32), vm((K, NL * B), F32),
            vm((2 * G, N2), F32),
            vm((S, G, N2), F32), vm((S, G, N2), F32), vm((G, N2), F32), vm((3 * S, G, N2), F32),
            vm((S, G, H), F32), vm((S, G, H), F32), vm((G, H), F32), vm((R, G, H), F32),
            vm((2 * G, R // 2 * H), F32), vm((G, H), F32), vm((3 * S, G, H), F32),
            vm((K, 3 * N2), F32), vm((K, 2 * H), F32),
            vm((NL, K, B), F32), *edge,
            vm((NL, B), F32), vm((NL, C1, H), F32), vm((NL, C1, H), F32), vm((C1, H), F32),
            vm((C1, H), F32), vm((NL, C1), jnp.int32), vm((NL, C1), jnp.int32),
            vm((1, C1), jnp.int32), vm((1, C1), jnp.int32), vm((P2, N2), F32), vm((P2, N2), F32),
            vm((NL, H), jnp.int32), vm((NL, 3 * N2, H), BF16),
            vm((NL, H, B), BF16), vm((NL, H, B), BF16),
            vm((NL, 256, B), BF16), vm((NL, 256, B), BF16), vm((G, H), F32),
            pltpu.SemaphoreType.DMA((10,)), pltpu.SemaphoreType.DMA((10,)),
            pltpu.SemaphoreType.DMA((10,)),
            pltpu.SemaphoreType.DMA((2, 2, NL)), pltpu.SemaphoreType.DMA((2, 2, NL)),
            pltpu.SemaphoreType.DMA((2, 4)), pltpu.SemaphoreType.DMA((2, 4)),
            pltpu.SemaphoreType.DMA((6,)), pltpu.SemaphoreType.DMA((6,)),
        ]
        return pl.pallas_call(
            functools.partial(kernel, S, R, NL, K, C1, P2, N2),
            out_shape=jax.ShapeDtypeStruct(args[0].shape, F32),
            in_specs=[pl.BlockSpec(memory_space=pl.ANY)] * len(args),
            out_specs=pl.BlockSpec(memory_space=pltpu.VMEM),
            scratch_shapes=scratch,
            compiler_params=pltpu.CompilerParams(
                collective_id=0, has_side_effects=True, vmem_limit_bytes=56 * 2**20),
        )(*args[:6], args[6].T, args[7], jnp.transpose(args[8], (1, 0, 2)), args[9].T)

    in_specs = (
        P("sub", "region", None, None),
        P("sub", "region", None, None),
        P("sub", "region", None, None),
        P("sub", "region", None),
        P("sub", "region", None),
        P("sub", "region", None),
        P(),
        P("region", "sub", None),
        P("region", None, None),
        P(None, "region"),
    )
    out_specs = P("sub", "region", None, None)
    return jax.shard_map(
        on_device, mesh=mesh, in_specs=in_specs, out_specs=out_specs, check_vma=False
    )
```

time: 49.4 us -> 40 us (0.81)
  local copies, waits for them, and re-layouts: 7.14 us -> 1.87 us
  Pallas kernels: 42 us -> 38 us
    unnamed x4 -> x1, local copies, waits for them, and re-layouts: 7.14 us -> 1.87 us
    pallas_call x1, Pallas kernels: 42 us -> 38 us  [on_device(): pl.pallas_call(functools.partial(kernel, S, R, NL, K, C1, P2, N2), out_sh...]
where the time goes in v2:
time: 40 us; the launch traced here: 39.9 us
  Pallas kernels  38 us (95%)
  local copies, waits for them, and re-layouts  1.87 us (5%)
    pallas_call x1, Pallas kernels, on_device(): pl.pallas_call(functools.partial(kernel, S, R, NL, K, C1, P2, N2), out_sh...  38 us
    unnamed x1, local copies, waits for them, and re-layouts  1.87 us

profile of v2, /device:TPU:1, one launch (start us, length us, event | category | flops | bytes accessed | tf_op | source)
XLA Modules:
  0.0 39.9 jit_solution(4403618789802219735)
XLA Ops:
  0.0 38.0 %shard_map.100 = f32[8,1,32,512]{3,2,1,0:T(8,128)} custom-call(f32[8,1,32,512]{3,2,1,0:T(8,128)} %pieces.1, f32[8,1,512,512]{3,2,1,0:T(8,128)} %local_inverse.1, f32[8,1,24,512]{3,2,1,0:T(8,128)} %basis.1, s32[8,1,128]{2,1,0:T(1,128)} %match_south.1, s32[8,1,128]{2,1,0:T(1,128)} %match_east.1, s32[8,1,24]{2,1,0:T(1,128)} %primal_index.1, s32[32,64]{1,0:T(8,128)} %bitcast.5, ...), custom_call_target="tpu_custom_call" | custom-call | tf_op jit(solution)/shard_map/pallas_call | solution.py:505
  38.0 1.9 %copy.12 = f32[8,1,32,512]{3,2,1,0:T(8,128)} copy(f32[8,1,32,512]{3,2,1,0:T(8,128)} %shard_map.100) | data formatting | bytes 1048576

commit v3 on v2

--- a/solution.py
+++ b/solution.py
@@ -8,7 +8,8 @@
 from jax.sharding import PartitionSpec as P
 
 H = 128
-EARLY = 4
+EARLY = 3
+X = 4
 MESH = pl.DeviceIdType.MESH
 F32 = jnp.float32
 BF16 = jnp.bfloat16
@@ -52,7 +53,7 @@
     comb, got_west2, got_east2, got_north2, got_south2,
     weight_near, bas_west, bas_east, bas_north, bas_south, index_west, index_east, index_north,
     index_south, l2_west, l2_east, slots, looks, big_b_high, big_b_low, big_q_high, big_q_low,
-    fix_rolled, more_send, more_recv,
+    fix_rolled, relay, more_send, more_recv,
     load_sem, edge_send, edge_recv, small_send, small_recv, step_send, step_recv,
 ):
     s = lax.axis_index("sub")
@@ -64,15 +65,22 @@
 
     barrier = pltpu.get_barrier_semaphore()
 
-    def tell_region(i, c):
-        pl.semaphore_signal(barrier, inc=1, device_id=(s, lax.rem(b + i, R)), device_id_type=MESH)
+    def tell(region, own=s):
+        pl.semaphore_signal(barrier, inc=1, device_id=(own, region), device_id_type=MESH)
+
+    def tell_sub(i, c):
+        tell(b, lax.rem(s + i, S))
         return c
 
-    def tell_sub(i, c):
-        for region in (b, east_of[1], west_of[1]):
+    up, down = lax.rem(b + X, R), lax.rem(b + R - X, R)
+
+    def relay_start(k, regions):
+        for region in regions:
             pl.semaphore_signal(
-                barrier, inc=1, device_id=(lax.rem(s + i, S), region), device_id_type=MESH)
-        return c
+                relay.at[k], inc=1, device_id=(s, region), device_id_type=MESH)
+
+    def relay_wait(k):
+        pl.semaphore_wait(relay.at[k], 2)
 
     own_rows = pl.ds(pl.multiple_of(s * OWN, 8), OWN)
     loads = [
@@ -87,11 +95,16 @@
         pltpu.make_async_copy(top_inverse, topt, load_sem.at[8]),
         pltpu.make_async_copy(local_inverse.at[:, 0], inv, load_sem.at[9]),
     ]
-    lax.fori_loop(1, R, tell_region, 0)
+    for region in (east_of[1], west_of[1], up, down):
+        tell(region)
+    for i in range(1, X):
+        tell(b // X * X + lax.rem(b + i, X))
     lax.fori_loop(1, S, tell_sub, 0)
     for load in loads:
         load.start()
-    pl.semaphore_wait(barrier, R - 1 + 3 * (S - 1))
+    pl.semaphore_wait(barrier, 4 + X - 1 + S - 1)
+    relay_start(0, (up, down))
+    relay_start(4, (east_of[1], west_of[1]))
 
     def remote(src, dst, send, recv, device):
         return pltpu.make_async_remote_copy(
@@ -164,6 +177,9 @@
     loads[1].wait()
     for a in range(NL - 1):
         unsouth[a] = invert(south[a:a + 1, :])
+
+    relay_wait(0)
+    relay_start(1, (up, down))
 
     loads[3].wait()
     levels = stiff[...].astype(F32)
@@ -205,6 +221,9 @@
         lbb_high[half, 4 * H * a:4 * H * (a + 1)] = high
         lbb_low[half, 4 * H * a:4 * H * (a + 1)] = low
 
+    relay_wait(1)
+    relay_start(2, (up, down))
+
     loads[8].wait()
     for c in range(R * P2 // 128):
         topv[128 * c:128 * (c + 1), :] = topt[:, 128 * c:128 * (c + 1)].T
@@ -224,6 +243,9 @@
     def masked(condition, value):
         return jnp.where(condition, value, jnp.zeros_like(value))
 
+    relay_wait(2)
+    relay_start(3, (up, down))
+
     table_south.wait_recv()
     unsouth[NL - 1] = invert(north_table[...])
     table_east.wait_recv()
@@ -240,6 +262,7 @@
         at = 4 * H * a
         asm[:, at:at + H] = pc[a, :, 0:H] + before
         asm[:, at + H:at + 2 * H] = pc[a, :, H:2 * H] + after
+    top = jnp.zeros((K, H), F32)
     for a in range(NL):
         at = 4 * H * a
         to_east(a).wait_recv()
@@ -248,8 +271,9 @@
         to_west(a).wait_recv()
         asm[:, at + 3 * H:at + 4 * H] = pc[a, :, 3 * H:] + masked(
             b < R - 1, pick(got_east[a], east[a:a + 1, :]))
-
-    top = three(nt, asm[...], lbb_high[...], lbb_low[...])
+        top += three(nt, asm[:, at:at + 4 * H], lbb_high[:, at:at + 4 * H],
+                     lbb_low[:, at:at + 4 * H])
+
     for g in range(S):
         top_sent[g] = top[G * g:G * (g + 1)]
 
@@ -295,6 +319,8 @@
         mine += top_got[g]
     cast_own[...] = mine
     cast_got[b] = mine
+
+    relay_wait(3)
 
     def cast(i, c):
         o = lax.rem(b + R // 2 + i, R)
@@ -322,6 +348,7 @@
     left = lhs_two[...].astype(BF16)
     first = nn(left, i_high)
     lift4 = first[0:G] + first[G:2 * G] + nn(left, i_low)[0:G]
+    relay_wait(4)
     lift_own[...] = lift4
     lift_got[s] = lift4
 
@@ -496,6 +523,7 @@
             vm((NL, H), jnp.int32), vm((NL, 3 * N2, H), BF16),
             vm((NL, H, B), BF16), vm((NL, H, B), BF16),
             vm((NL, 256, B), BF16), vm((NL, 256, B), BF16), vm((G, H), F32),
+            pltpu.SemaphoreType.REGULAR((5,)),
             pltpu.SemaphoreType.DMA((10,)), pltpu.SemaphoreType.DMA((10,)),
             pltpu.SemaphoreType.DMA((10,)),
             pltpu.SemaphoreType.DMA((2, 2, NL)), pltpu.SemaphoreType.DMA((2, 2, NL)),

time: 40 us -> 37.5 us (0.938)
  Pallas kernels: 38 us -> 35.5 us
    pallas_call x1, Pallas kernels: 38 us -> 35.5 us  [on_device(): pl.pallas_call(functools.partial(kernel, S, R, NL, K, C1, P2, N2), out_sh...]
where the time goes in v3:
time: 37.5 us; the launch traced here: 37.4 us
  Pallas kernels  35.5 us (95%)
  local copies, waits for them, and re-layouts  1.87 us (5%)
    pallas_call x1, Pallas kernels, on_device(): pl.pallas_call(functools.partial(kernel, S, R, NL, K, C1, P2, N2), out_sh...  35.5 us
    unnamed x1, local copies, waits for them, and re-layouts  1.87 us

profile of v3, /device:TPU:1, one launch (start us, length us, event | category | flops | bytes accessed | tf_op | source)
XLA Modules:
  0.0 37.4 jit_solution(11991788703173374409)
XLA Ops:
  0.0 35.5 %shard_map.100 = f32[8,1,32,512]{3,2,1,0:T(8,128)} custom-call(f32[8,1,32,512]{3,2,1,0:T(8,128)} %pieces.1, f32[8,1,512,512]{3,2,1,0:T(8,128)} %local_inverse.1, f32[8,1,24,512]{3,2,1,0:T(8,128)} %basis.1, s32[8,1,128]{2,1,0:T(1,128)} %match_south.1, s32[8,1,128]{2,1,0:T(1,128)} %match_east.1, s32[8,1,24]{2,1,0:T(1,128)} %primal_index.1, s32[32,64]{1,0:T(8,128)} %bitcast.5, ...), custom_call_target="tpu_custom_call" | custom-call | tf_op jit(solution)/shard_map/pallas_call | solution.py:533
  35.5 1.9 %copy.12 = f32[8,1,32,512]{3,2,1,0:T(8,128)} copy(f32[8,1,32,512]{3,2,1,0:T(8,128)} %shard_map.100) | data formatting | bytes 1048576

commit v4 on v3

--- a/solution.py
+++ b/solution.py
@@ -8,7 +8,7 @@
 from jax.sharding import PartitionSpec as P
 
 H = 128
-EARLY = 3
+EARLY = 2
 X = 4
 MESH = pl.DeviceIdType.MESH
 F32 = jnp.float32
@@ -357,16 +357,16 @@
         remote(rolled, got.at[S + s], step_send.at[k], step_recv.at[k], (o, east_of[1])).start()
         remote(src, got.at[2 * S + s], step_send.at[k], step_recv.at[k], (o, west_of[1])).start()
 
-    def to_three_regions(src, rolled, got, k):
+    def to_three_regions(src, rolled, got, k, k_near):
         def body(i, c):
-            spread(i, src, rolled, got, k)
+            spread(i, src, rolled, got, k_near)
             o = lax.rem(s + i, S)
             remote(src, got.at[s], step_send.at[k], step_recv.at[k], (o, b)).start()
             return c
         lax.fori_loop(1, S, body, 0)
-        spread(0, src, rolled, got, k)
-
-    to_three_regions(lift_own, lift_own, lift_got, 4)
+        spread(0, src, rolled, got, k_near)
+
+    to_three_regions(lift_own, lift_own, lift_got, 4, 4)
 
     for copy in more:
         copy.wait_recv()
@@ -434,7 +434,7 @@
     fix = fix_own[...]
     fix_rolled[...] = pltpu.roll(fix, 64, 1)
     fix_got[s] = fix
-    to_three_regions(fix_own, fix_rolled, fix_got, 5)
+    to_three_regions(fix_own, fix_rolled, fix_got, 5, 6)
 
     to_north2.wait_recv()
     to_south2.wait_recv()
@@ -460,16 +460,28 @@
         at = 4 * H * a
         fixed[:, at:at + 4 * H] += three(nn, e[:K] + e[K:], big_b_high[a], big_b_low[a])
 
-    arrived(fix_got, 3 * S - 1, step_recv.at[5])
+    arrived(fix_got, S - 1, step_recv.at[5])
     for g in range(S):
-        tf[G * g:G * (g + 1), 0:H] = fix_got[g] + fix_got[S + g]
+        tf[G * g:G * (g + 1), 0:H] = fix_got[g]
+    f_high, f_low = split(tf[:, 0:H])
+    f_both = jnp.concatenate([f_high, f_low], axis=0)
+    for a in range(NL):
+        both = nn(f_both, big_q_high[a, 0:H, :])
+        value = fixed[:, 4 * H * a:4 * H * (a + 1)] + both[:K] + both[K:] + nn(
+            f_high, big_q_low[a, 0:H, :])
+        out[a, 0, :, 0:2 * H] = value[:, 0:2 * H]
+        fixed[:, 4 * H * a + 2 * H:4 * H * (a + 1)] = value[:, 2 * H:]
+
+    arrived(fix_got, 2 * S, step_recv.at[6])
+    for g in range(S):
+        tf[G * g:G * (g + 1), 0:H] = fix_got[S + g]
         tf[G * g:G * (g + 1), H:2 * H] = fix_got[2 * S + g]
     f_high, f_low = split(tf[...])
     f_both = jnp.concatenate([f_high, f_low], axis=0)
     for a in range(NL):
-        both = nn(f_both, big_q_high[a])
-        out[a, 0] = fixed[:, 4 * H * a:4 * H * (a + 1)] + both[:K] + both[K:] + nn(
-            f_high, big_q_low[a])
+        both = nn(f_both, big_q_high[a, :, 2 * H:])
+        out[a, 0, :, 2 * H:] = fixed[:, 4 * H * a + 2 * H:4 * H * (a + 1)] + both[:K] + both[
+            K:] + nn(f_high, big_q_low[a, :, 2 * H:])
 
     for first in ((to_west, to_east, to_north, to_south),
                   (to_west2, to_east2, to_north2, to_south2)):
@@ -487,7 +499,8 @@
     arrived(cast_got, R - 1, step_send.at[2])
     arrived(l2inv, (S - 1) * OWN, step_send.at[3])
     arrived(lift_got, 3 * S - 1, step_send.at[4])
-    arrived(fix_got, 3 * S - 1, step_send.at[5])
+    arrived(fix_got, S - 1, step_send.at[5])
+    arrived(fix_got, 2 * S, step_send.at[6])
 
 
 def solution(mesh):
@@ -528,7 +541,7 @@
             pltpu.SemaphoreType.DMA((10,)),
             pltpu.SemaphoreType.DMA((2, 2, NL)), pltpu.SemaphoreType.DMA((2, 2, NL)),
             pltpu.SemaphoreType.DMA((2, 4)), pltpu.SemaphoreType.DMA((2, 4)),
-            pltpu.SemaphoreType.DMA((6,)), pltpu.SemaphoreType.DMA((6,)),
+            pltpu.SemaphoreType.DMA((7,)), pltpu.SemaphoreType.DMA((7,)),
         ]
         return pl.pallas_call(
             functools.partial(kernel, S, R, NL, K, C1, P2, N2),

time: 37.5 us -> 37.1 us (0.989)
  Pallas kernels: 35.5 us -> 35.1 us
    pallas_call x1, Pallas kernels: 35.5 us -> 35.1 us  [on_device(): pl.pallas_call(functools.partial(kernel, S, R, NL, K, C1, P2, N2), out_sh...]
where the time goes in v4:
time: 37.1 us; the launch traced here: 37 us
  Pallas kernels  35.1 us (95%)
  local copies, waits for them, and re-layouts  1.87 us (5%)
    pallas_call x1, Pallas kernels, on_device(): pl.pallas_call(functools.partial(kernel, S, R, NL, K, C1, P2, N2), out_sh...  35.1 us
    unnamed x1, local copies, waits for them, and re-layouts  1.87 us

profile of v4, /device:TPU:1, one launch (start us, length us, event | category | flops | bytes accessed | tf_op | source)
XLA Modules:
  0.0 37.0 jit_solution(6213120731919678036)
XLA Ops:
  0.0 35.1 %shard_map.100 = f32[8,1,32,512]{3,2,1,0:T(8,128)} custom-call(f32[8,1,32,512]{3,2,1,0:T(8,128)} %pieces.1, f32[8,1,512,512]{3,2,1,0:T(8,128)} %local_inverse.1, f32[8,1,24,512]{3,2,1,0:T(8,128)} %basis.1, s32[8,1,128]{2,1,0:T(1,128)} %match_south.1, s32[8,1,128]{2,1,0:T(1,128)} %match_east.1, s32[8,1,24]{2,1,0:T(1,128)} %primal_index.1, s32[32,64]{1,0:T(8,128)} %bitcast.5, ...), custom_call_target="tpu_custom_call" | custom-call | tf_op jit(solution)/shard_map/pallas_call | solution.py:546
  35.1 1.9 %copy.12 = f32[8,1,32,512]{3,2,1,0:T(8,128)} copy(f32[8,1,32,512]{3,2,1,0:T(8,128)} %shard_map.100) | data formatting | bytes 1048576

commit v5 on v4

--- a/solution.py
+++ b/solution.py
@@ -323,13 +323,12 @@
     relay_wait(3)
 
     def cast(i, c):
-        o = lax.rem(b + R // 2 + i, R)
-
+        o = lax.rem(b + i, R)
         remote(cast_own, cast_got.at[b], step_send.at[2], step_recv.at[2], (s, o)).start()
         return c
 
-    lax.fori_loop(0, R // 2, cast, 0)
-    lax.fori_loop(R // 2 + 1, R, cast, 0)
+    for i in sorted(range(1, R), key=lambda i: (abs(R // 2 - i), i)):
+        cast(i, 0)
 
     lax.fori_loop(EARLY, NL, solve, 0)
     to_north2.start()
@@ -363,7 +362,8 @@
             o = lax.rem(s + i, S)
             remote(src, got.at[s], step_send.at[k], step_recv.at[k], (o, b)).start()
             return c
-        lax.fori_loop(1, S, body, 0)
+        for i in sorted(range(1, S), key=lambda i: (abs(S // 2 - i), i)):
+            body(i, 0)
         spread(0, src, rolled, got, k_near)
 
     to_three_regions(lift_own, lift_own, lift_got, 4, 4)

time: 37.1 us -> 36.8 us (level)
  no operation moved by 1% of the time
where the time goes in v5:
time: 36.8 us; the launch traced here: 36.7 us
  Pallas kernels  34.8 us (95%)
  local copies, waits for them, and re-layouts  1.87 us (5%)
    pallas_call x1, Pallas kernels, on_device(): pl.pallas_call(functools.partial(kernel, S, R, NL, K, C1, P2, N2), out_sh...  34.8 us
    unnamed x1, local copies, waits for them, and re-layouts  1.87 us

profile of v5, /device:TPU:1, one launch (start us, length us, event | category | flops | bytes accessed | tf_op | source)
XLA Modules:
  0.0 36.7 jit_solution(10714725102949906107)
XLA Ops:
  0.0 34.8 %shard_map.100 = f32[8,1,32,512]{3,2,1,0:T(8,128)} custom-call(f32[8,1,32,512]{3,2,1,0:T(8,128)} %pieces.1, f32[8,1,512,512]{3,2,1,0:T(8,128)} %local_inverse.1, f32[8,1,24,512]{3,2,1,0:T(8,128)} %basis.1, s32[8,1,128]{2,1,0:T(1,128)} %match_south.1, s32[8,1,128]{2,1,0:T(1,128)} %match_east.1, s32[8,1,24]{2,1,0:T(1,128)} %primal_index.1, s32[32,64]{1,0:T(8,128)} %bitcast.5, ...), custom_call_target="tpu_custom_call" | custom-call | tf_op jit(solution)/shard_map/pallas_call | solution.py:546
  34.8 1.9 %copy.12 = f32[8,1,32,512]{3,2,1,0:T(8,128)} copy(f32[8,1,32,512]{3,2,1,0:T(8,128)} %shard_map.100) | data formatting | bytes 1048576

commit v6 on v5

--- a/solution.py
+++ b/solution.py
@@ -142,10 +142,8 @@
     to_south.start()
 
     def others(count, me, make):
-        def body(i, c):
+        for i in sorted(range(1, count), key=lambda i: (abs(count // 2 - i), i)):
             make(lax.rem(me + i, count)).start()
-            return c
-        lax.fori_loop(1, count, body, 0)
 
     others(S, s, lambda o: remote(
         level2_inverse.at[0], l2inv.at[own_rows], step_send.at[3], step_recv.at[3], (o, b)))

time: 36.8 us -> 36.8 us (level)
  no operation moved by 1% of the time
where the time goes in v6:
time: 36.8 us; the launch traced here: 36.7 us
  Pallas kernels  34.8 us (95%)
  local copies, waits for them, and re-layouts  1.87 us (5%)
    pallas_call x1, Pallas kernels, on_device(): pl.pallas_call(functools.partial(kernel, S, R, NL, K, C1, P2, N2), out_sh...  34.8 us
    unnamed x1, local copies, waits for them, and re-layouts  1.87 us

profile of v6, /device:TPU:1, one launch (start us, length us, event | category | flops | bytes accessed | tf_op | source)
XLA Modules:
  0.0 36.7 jit_solution(455704761249939212)
XLA Ops:
  0.0 34.8 %shard_map.100 = f32[8,1,32,512]{3,2,1,0:T(8,128)} custom-call(f32[8,1,32,512]{3,2,1,0:T(8,128)} %pieces.1, f32[8,1,512,512]{3,2,1,0:T(8,128)} %local_inverse.1, f32[8,1,24,512]{3,2,1,0:T(8,128)} %basis.1, s32[8,1,128]{2,1,0:T(1,128)} %match_south.1, s32[8,1,128]{2,1,0:T(1,128)} %match_east.1, s32[8,1,24]{2,1,0:T(1,128)} %primal_index.1, s32[32,64]{1,0:T(8,128)} %bitcast.5, ...), custom_call_target="tpu_custom_call" | custom-call | tf_op jit(solution)/shard_map/pallas_call | solution.py:544
  34.8 1.9 %copy.12 = f32[8,1,32,512]{3,2,1,0:T(8,128)} copy(f32[8,1,32,512]{3,2,1,0:T(8,128)} %shard_map.100) | data formatting | bytes 1048576
